TPU v7x, 256 devices: a whole 4x4x8 slice. The times are simulated.
256 devices in a mesh: own: 8 (over z), col: 8 (over x, core), mlp: 4 (over y).
Axes of the slice: x: 4, y: 4, z: 8, core: 2. Of those that a mesh axis runs over, the one named last changes fastest.
Arguments:
- features: bfloat16 [262144, 512], P(('own', 'col')), may hold values from -6 to 6
- nbr_page: int32 [8192, 32], P(('own', 'col')), may hold values from 0 to 262143, as said below
- nbr_weight: bfloat16 [8192, 32], P(('own', 'col')), may hold values from 0.0049743652 to 0.29882812
- labels: int32 [8192], P(('own', 'col')), may hold values from 0 to 255
- w_one: bfloat16 [512, 2048], P(None, 'mlp'), may hold values from -0.25 to 0.25
- w_two: bfloat16 [2048, 256], P('mlp'), may hold values from -0.125 to 0.125
Outputs:
- grad_one: float32 [512, 2048], P(None, 'mlp')
- grad_two: float32 [2048, 256], P('mlp')
Inputs may be any that keep to these rules, and one draw needn't show every extreme that they name: `nbr_page`: page p is held by owner p // 4096 (owners numbered along own then col) at its row p % 4096. The 32 neighbours of a target are distinct pages listed in non-decreasing order of owner. Of the 4096 neighbour entries of the targets of one index of own and col, at most 128 fall on one owner; one owner receives exactly 128 entries from every index, and some owners receive none from some indices.
All inputs are finite; a program needn't handle non-finite values.
Results may differ from a plain program's by a relative error of at most 0.011.
Values may be sent and summed in bfloat16 or wider, within the bound.
No kernel may reach another device: no remote copies, remote signals or barrier semaphores. Data moves between devices by JAX's collectives and lax.ppermute only.
A program may use at most 128 MiB of HBM per device.

v0:
```python
import jax
import jax.numpy as jnp
from jax import lax
from jax.sharding import PartitionSpec as P


def body(features, nbr_page, nbr_weight, labels, w_one, w_two):
    rows_dev = features.shape[0]
    width_f = features.shape[1]
    targets = nbr_page.shape[0]
    width_k = nbr_page.shape[1]
    owners = lax.axis_size(("own", "col"))
    entries = targets * width_k
    capacity = 2 * entries // owners
    owner_ids = nbr_page // rows_dev
    local_row = nbr_page % rows_dev
    owner_range = jnp.arange(owners, dtype=jnp.int32)
    matches = (owner_ids[:, :, None] == owner_range[None, None, :]).astype(jnp.int32)
    row_count = jnp.sum(matches, axis=1)
    earlier_rows = jnp.cumsum(row_count, axis=0) - row_count
    before_owner = jnp.cumsum(row_count, axis=1) - row_count
    first_slot = earlier_rows - before_owner + owner_range[None, :] * capacity
    slot_ids = (
        jnp.sum(matches * first_slot[:, None, :], axis=2)
        + jnp.arange(width_k, dtype=jnp.int32)[None, :]
    )
    flat_slot = slot_ids.reshape(-1)
    requests = jnp.zeros((owners * capacity,), jnp.int32).at[flat_slot].set(local_row.reshape(-1))
    requests = requests.reshape(owners, capacity)
    asked_rows = lax.all_to_all(requests, ("own", "col"), split_axis=0, concat_axis=0, tiled=True)
    fetched = features[asked_rows]
    returned = lax.all_to_all(fetched, ("own", "col"), split_axis=0, concat_axis=0, tiled=True)
    received = returned.reshape(owners * capacity, width_f)
    contract_first = (((0,), (0,)), ((), ()))
    target_ids = jnp.broadcast_to(
        jnp.arange(targets, dtype=jnp.int32)[:, None], (targets, width_k)
    ).reshape(-1)
    spread = (
        jnp.zeros((targets, owners * capacity), jnp.bfloat16)
        .at[target_ids, flat_slot]
        .set(nbr_weight.reshape(-1))
    )
    pre_act = jnp.dot(received, w_one, preferred_element_type=jnp.float32)
    active = jnp.maximum(pre_act, 0.0).astype(jnp.bfloat16)
    hidden = jnp.dot(spread, active, preferred_element_type=jnp.float32).astype(jnp.bfloat16)
    partial_logits = jnp.dot(hidden, w_two, preferred_element_type=jnp.float32)
    logits = lax.psum(partial_logits, "mlp")
    exponent = jnp.exp(logits)
    probability = exponent / jnp.sum(exponent, axis=1, keepdims=True)
    classes = w_two.shape[1]
    onehot_label = (labels[:, None] == jnp.arange(classes, dtype=jnp.int32)[None, :]).astype(
        jnp.float32
    )
    d_logits = (probability - onehot_label).astype(jnp.bfloat16)
    grad_two = lax.dot_general(hidden, d_logits, contract_first, preferred_element_type=jnp.float32)
    d_hidden = lax.dot_general(
        d_logits, w_two, (((1,), (1,)), ((), ())), preferred_element_type=jnp.float32
    ).astype(jnp.bfloat16)
    positive = (pre_act > 0).astype(jnp.float32)
    scattered = lax.dot_general(
        spread, d_hidden, contract_first, preferred_element_type=jnp.float32
    )
    d_pre = (scattered * positive).astype(jnp.bfloat16)
    grad_one = lax.dot_general(received, d_pre, contract_first, preferred_element_type=jnp.float32)
    grad_one, grad_two = lax.psum((grad_one, grad_two), ("own", "col"))
    return (grad_one, grad_two)


def solution(mesh):
    placed = (
        P(("own", "col"), None),
        P(("own", "col"), None),
        P(("own", "col"), None),
        P(("own", "col")),
        P(None, "mlp"),
        P("mlp", None),
    )
    return jax.shard_map(
        body,
        mesh=mesh,
        in_specs=placed,
        out_specs=(P(None, "mlp"), P("mlp", None)),
        check_vma=False,
    )
```

profile of v0, /device:TPU:8, one launch (start us, length us, event | category | flops | bytes accessed | tf_op | source)
XLA Modules:
  0.0 551.1 jit_solution(711926448814235918)
XLA Ops:
  7.2 0.0 copy-start
  7.2 0.8 add_select_fusion
  8.0 0.1 convert_reduce_fusion
  8.1 0.1 copy.16
  8.2 0.1 reduce_window_sum.23
  8.3 0.1 copy.18
  8.4 0.1 copy.22
  8.5 0.1 reshape.163
  8.6 0.2 reduce_window_sum.22
  8.8 0.1 copy.20
  8.8 0.2 select_reduce_fusion
  9.1 0.1 copy.21
  9.2 0.1 add.85
  9.3 0.1 reshape.145
  9.4 15.5 %scatter_custom_fusion = s32[8192]{0:T(1024)S(1)} fusion(s32[4096]{0:T(1024)S(1)} %bitcast.22, s32[4096]{0:T(1024)S(1)} %reshape.163, s32[]{:T(128)} %constant.41.clone.1), kind=kCustom, calls=%fused_computation.34 | custom fusion | bytes 32772 | tf_op jit(solution)/shard_map/scatter | solution.py:28
  25.0 21.3 %all_to_all.17 = s32[64,1,128]{2,1,0:T(1,128)S(1)} all-to-all(s32[64,1,128]{2,1,0:T(1,128)S(1)} %bitcast.23), channel_id=1, replica_groups=mesh['own'=8,'col'=8,'mlp'=4] {'own','col'}, dimensions={0} | all-to-all | bytes 65536 | tf_op jit(solution)/shard_map/all_to_all | solution.py:30
  46.3 36.5 %gather_fusion = bf16[8192,512]{1,0:T(8,128)(2,1)} fusion(bf16[4096,512]{1,0:T(8,128)(2,1)} %param.6, s32[8192]{0:T(1024)S(1)} %fusion.7), kind=kCustom, calls=%fused_computation | custom fusion | bytes 16809984 | tf_op jit(solution)/shard_map/gather | solution.py:31
  82.8 5.9 %all-to-all-start.1 = ((bf16[64,128,512]{2,1,0:T(8,128)(2,1)}), bf16[64,128,512]{2,1,0:T(8,128)(2,1)}, u32[]{:S(2)}, u32[]{:S(2)}) async-start(bf16[64,128,512]{2,1,0:T(8,128)(2,1)} %bitcast.21), calls=%async_computation.1 | async-start | bytes 16777216 | tf_op jit(solution)/shard_map/all_to_all | solution.py:32
  88.7 0.0 all-reduce.4.cloned.1.call-start
  88.8 0.0 copy-done.4
  88.8 0.1 copy.23
  88.9 0.1 reshape.169
  89.0 0.0 copy-done.7
  89.0 0.1 multiply_reduce_fusion
  89.1 0.0 copy-done.6
  89.1 0.1 and_reduce_fusion
  89.3 30.4 %scatter_custom_fusion.1 = bf16[1048576]{0:T(1024)(128)(2,1)} fusion(s32[4096]{0:T(1024)S(1)} %broadcast_select_fusion, bf16[4096]{0:T(1024)(128)(2,1)S(1)} %reshape.169, bf16[]{:T(256)} %constant.50.clone.1), kind=kCustom, calls=%fused_computation.10 | custom fusion | bytes 2097154
  119.7 2.8 reshape.150
  122.5 152.3 %all-to-all-done.1 = bf16[64,128,512]{2,1,0:T(8,128)(2,1)} async-done(((bf16[64,128,512]{2,1,0:T(8,128)(2,1)}), bf16[64,128,512]{2,1,0:T(8,128)(2,1)}, u32[]{:S(2)}, u32[]{:S(2)}) %all-to-all-start.1) | async-done | bytes 8388640 | tf_op jit(solution)/shard_map/all_to_all | solution.py:32
  274.8 0.0 copy-done
  274.8 7.1 %fusion.15 = f32[8192,512]{1,0:T(8,128)S(1)} fusion(bf16[8192,512]{1,0:T(8,128)(2,1)} %bitcast.5, bf16[512,512]{1,0:T(8,128)(2,1)S(1)} %copy-done), kind=kOutput, calls=%fused_computation.43 | convolution fusion | flops 4294967296 | bytes 25690112 | tf_op jit(solution)/shard_map/dot_general | solution.py:43
  281.9 0.0 copy-start.3
  281.9 0.0 copy-start.5
  281.9 1.6 fusion.3
  283.5 4.1 copy-done.1
  287.6 0.8 fusion.16
  288.4 0.0 all-reduce.4.cloned.1.call-update
  288.5 0.0 all-reduce.6.cloned.1.call-start
  288.5 42.6 %all-reduce.4.cloned.1.call-done = f32[128,256]{1,0:T(8,128)} async-done(((f32[128,256]{1,0:T(8,128)}), f32[128,256]{1,0:T(8,128)}) %all-reduce.4.cloned.1.call-update) | async-done | bytes 131088 | tf_op jit(solution)/shard_map/psum | solution.py:47
  331.1 1.0 exponential_reduce_fusion
  332.1 0.0 copy-done.5
  332.1 1.1 convolution_convert_fusion
  333.2 16.1 %fusion.2 = f32[512,512]{1,0:T(8,128)} fusion(bf16[8192,512]{1,0:T(8,128)(2,1)} %bitcast.5, f32[8192,512]{1,0:T(8,128)} %copy-done.1, bf16[128,8192]{1,0:T(8,128)(2,1)S(1)} %reshape.150, bf16[128,512]{1,0:T(8,128)(2,1)S(1)} %convolution_convert_fusion), kind=kOutput, calls=%fused_computation.7 | convolution fusion | flops 5381292032 | bytes 28442624 | tf_op jit(solution)/shard_map/dot_general | solution.py:64
  349.3 1.1 fusion.14
  350.4 0.0 all-reduce.6.cloned.1.call-update
  350.5 189.7 %all-reduce.6.cloned.1.call-done = (f32[512,512]{1,0:T(8,128)}, f32[512,256]{1,0:T(8,128)}) async-done(((f32[512,512]{1,0:T(8,128)}, f32[512,256]{1,0:T(8,128)}), (f32[512,512]{1,0:T(8,128)}, f32[512,256]{1,0:T(8,128)})) %all-reduce.6.cloned.1.call-update) | async-done | bytes 1572880 | tf_op jit(solution)/shard_map/psum | solution.py:65
  540.2 2.3 copy.27
  542.4 1.9 copy.28
  (14 shorter events, 0.1 us)
Async XLA Ops:
  7.2 267.6 %copy-start = (bf16[512,512]{1,0:T(8,128)(2,1)S(1)}, bf16[512,512]{1,0:T(8,128)(2,1)}, u32[]{:S(2)}) copy-start(bf16[512,512]{1,0:T(8,128)(2,1)} %param.10) | copy-start | bytes 1572868
  82.8 6.0 %copy-start.4 = (bf16[128,32]{0,1:T(8,128)(2,1)S(1)}, bf16[128,32]{0,1:T(8,128)(2,1)}, u32[]{:S(2)}) copy-start(bf16[128,32]{0,1:T(8,128)(2,1)} %param.8) | copy-start | bytes 24580
  82.8 6.2 %copy-start.7 = (s32[2]{0:T(128)S(1)}, s32[2]{0:T(128)}, u32[]{:S(2)}) copy-start(s32[2]{0:T(128)} %constant.51) | copy-start | bytes 28
  82.8 6.3 %copy-start.6 = (s32[2]{0:T(128)S(1)}, s32[2]{0:T(128)}, u32[]{:S(2)}) copy-start(s32[2]{0:T(128)} %constant.54) | copy-start | bytes 28
  82.8 191.9 %all-to-all-start.1 = ((bf16[64,128,512]{2,1,0:T(8,128)(2,1)}), bf16[64,128,512]{2,1,0:T(8,128)(2,1)}, u32[]{:S(2)}, u32[]{:S(2)}) async-start(bf16[64,128,512]{2,1,0:T(8,128)(2,1)} %bitcast.21), calls=%async_computation.1 | async-start | bytes 16777216 | tf_op jit(solution)/shard_map/all_to_all | solution.py:32
  88.7 242.3 %all-reduce.4.cloned.1.call-start = ((), (), s32[]{:S(2)}) async-start(), calls=%async_computation.2 | async-start | bytes 262144 | tf_op jit(solution)/shard_map/psum | solution.py:47
  281.9 5.7 %copy-start.1 = (f32[8192,512]{1,0:T(8,128)}, f32[8192,512]{1,0:T(8,128)S(1)}, u32[]{:S(2)}) copy-start(f32[8192,512]{1,0:T(8,128)S(1)} %fusion.15) | copy-start | bytes 50331652
  281.9 5.7 %copy-start.3 = (bf16[512,256]{1,0:T(8,128)(2,1)S(1)}, bf16[512,256]{1,0:T(8,128)(2,1)}, u32[]{:S(2)}) copy-start(bf16[512,256]{1,0:T(8,128)(2,1)} %param.11) | copy-start | bytes 786436
  281.9 50.2 %copy-start.5 = (s32[128]{0:T(128)S(1)}, s32[128]{0:T(128)}, u32[]{:S(2)}) copy-start(s32[128]{0:T(128)} %param.9) | copy-start | bytes 1540
  288.5 251.7 %all-reduce.6.cloned.1.call-start = ((), (), s32[]{:S(2)}) async-start(), calls=%async_computation.3 | async-start | bytes 3145728 | tf_op jit(solution)/shard_map/psum | solution.py:65
  333.2 16.1 %copy-start.2 = (f32[128,256]{1,0:T(8,128)S(1)}, f32[128,256]{1,0:T(8,128)}, u32[]{:S(2)}) copy-start(f32[128,256]{1,0:T(8,128)} %all-reduce.4.cloned.1.call-done) | copy-start | bytes 393220
Sparse Core Ops, SparseCore 0:
  288.6 42.4 all-reduce.3
  350.6 189.5 all-reduce.5
where the time goes:
time: 552 us; the launch traced here: 551 us
  waiting for transfers between devices  385 us (70%)
  local copies, waits for them, and re-layouts  94.5 us (17%)
  matrix products  27.8 us (5%)
  blocking collectives  21.3 us (4%)
  between operations  14.3 us (3%)
  starting transfers between devices  5.97 us (1%)
    psum x1, waiting for transfers between devices, body(): grad_one, grad_two = lax.psum((grad_one, grad_two), ('own', 'col'))  190 us
    all_to_all x1, waiting for transfers between devices, body(): lax.all_to_all(fetched, ('own', 'col'), split_axis=0, concat_axis=0, tile...  152 us
    psum x1, waiting for transfers between devices, body(): logits = lax.psum(partial_logits, 'mlp')  42.6 us
    unnamed x20, local copies, waits for them, and re-layouts  38.8 us
    gather x1, local copies, waits for them, and re-layouts, body(): fetched = features[asked_rows]  36.5 us
    all_to_all x1, blocking collectives, body(): lax.all_to_all(requests, ('own', 'col'), split_axis=0, concat_axis=0, til...  21.3 us
    dot_general x1, matrix products, body(): lax.dot_general(received, d_pre, contract_first, preferred_element_type=j...  16.1 us
    scatter x1, local copies, waits for them, and re-layouts, body(): jnp.zeros((owners * capacity,), jnp.int32).at[flat_slot]  15.5 us
  transfers between devices with their start and end apart: 3, of which 3 were waited for; matrix products, arithmetic and copies ran while one was open for 6% of the time, Pallas kernels for 0%

commit v1 on v0

--- a/solution.py
+++ b/solution.py
@@ -2,6 +2,11 @@
 import jax.numpy as jnp
 from jax import lax
 from jax.sharding import PartitionSpec as P
+
+
+def axis_by_axis(value, inner_axis, outer_axis):
+    half = lax.psum(value, inner_axis)
+    return lax.psum(half, outer_axis)
 
 
 def body(features, nbr_page, nbr_weight, labels, w_one, w_two):
@@ -62,7 +67,7 @@
     )
     d_pre = (scattered * positive).astype(jnp.bfloat16)
     grad_one = lax.dot_general(received, d_pre, contract_first, preferred_element_type=jnp.float32)
-    grad_one, grad_two = lax.psum((grad_one, grad_two), ("own", "col"))
+    grad_one, grad_two = axis_by_axis((grad_one, grad_two), "col", "own")
     return (grad_one, grad_two)
 
 

time: 552 us -> 513 us (0.929)
  waiting for transfers between devices: 385 us -> 347 us
    psum x1 -> x2, waiting for transfers between devices: 190 us -> 152 us  [the longest x1 80.8 us: axis_by_axis(): return lax.psum(half, outer_axis)]
  transfers between devices with their start and end apart: 3 -> 4, of which waited for: 3 -> 4; matrix products, arithmetic and copies ran while one was open for 6% -> 7% of each run, Pallas kernels for 0% -> 0%
where the time goes in v1:
time: 513 us
  waiting for transfers between devices  347 us (68%)
  local copies, waits for them, and re-layouts  94.5 us (18%)
  matrix products  27.8 us (5%)
  blocking collectives  21.3 us (4%)
  between operations  14 us (3%)
  starting transfers between devices  6.01 us (1%)
    all_to_all x1, waiting for transfers between devices, body(): lax.all_to_all(fetched, ('own', 'col'), split_axis=0, concat_axis=0, tile...  152 us
    psum x1, waiting for transfers between devices, axis_by_axis(): return lax.psum(half, outer_axis)  80.8 us
    psum x1, waiting for transfers between devices, axis_by_axis(): half = lax.psum(value, inner_axis)  70.9 us
    psum x1, waiting for transfers between devices, body(): logits = lax.psum(partial_logits, 'mlp')  42.6 us
    unnamed x20, local copies, waits for them, and re-layouts  38.8 us
    gather x1, local copies, waits for them, and re-layouts, body(): fetched = features[asked_rows]  36.5 us
    all_to_all x1, blocking collectives, body(): lax.all_to_all(requests, ('own', 'col'), split_axis=0, concat_axis=0, til...  21.3 us
    dot_general x1, matrix products, body(): lax.dot_general(received, d_pre, contract_first, preferred_element_type=j...  16.1 us
  transfers between devices with their start and end apart: 4, of which 4 were waited for; matrix products, arithmetic and copies ran while one was open for 7% of the time, Pallas kernels for 0%

profile of v1, /device:TPU:8, one launch (start us, length us, event | category | flops | bytes accessed | tf_op | source)
XLA Modules:
  0.0 512.9 jit_solution(6544283634433122361)
XLA Ops:
  7.2 0.0 copy-start
  7.2 0.8 add_select_fusion
  8.0 0.1 convert_reduce_fusion
  8.1 0.1 copy.16
  8.2 0.1 reduce_window_sum.23
  8.3 0.1 copy.18
  8.4 0.1 copy.22
  8.5 0.1 reshape.163
  8.6 0.2 reduce_window_sum.22
  8.8 0.1 copy.20
  8.8 0.2 select_reduce_fusion
  9.1 0.1 copy.21
  9.2 0.1 add.89
  9.3 0.1 reshape.145
  9.4 15.5 %scatter_custom_fusion = s32[8192]{0:T(1024)S(1)} fusion(s32[4096]{0:T(1024)S(1)} %bitcast.22, s32[4096]{0:T(1024)S(1)} %reshape.163, s32[]{:T(128)} %constant.41.clone.1), kind=kCustom, calls=%fused_computation.34 | custom fusion | bytes 32772 | tf_op jit(solution)/shard_map/scatter | solution.py:33
  25.0 21.3 %all_to_all.17 = s32[64,1,128]{2,1,0:T(1,128)S(1)} all-to-all(s32[64,1,128]{2,1,0:T(1,128)S(1)} %bitcast.23), channel_id=1, replica_groups=mesh['own'=8,'col'=8,'mlp'=4] {'own','col'}, dimensions={0} | all-to-all | bytes 65536 | tf_op jit(solution)/shard_map/all_to_all | solution.py:35
  46.3 36.5 %gather_fusion = bf16[8192,512]{1,0:T(8,128)(2,1)} fusion(bf16[4096,512]{1,0:T(8,128)(2,1)} %param.6, s32[8192]{0:T(1024)S(1)} %fusion.7), kind=kCustom, calls=%fused_computation | custom fusion | bytes 16809984 | tf_op jit(solution)/shard_map/gather | solution.py:36
  82.8 5.9 %all-to-all-start.1 = ((bf16[64,128,512]{2,1,0:T(8,128)(2,1)}), bf16[64,128,512]{2,1,0:T(8,128)(2,1)}, u32[]{:S(2)}, u32[]{:S(2)}) async-start(bf16[64,128,512]{2,1,0:T(8,128)(2,1)} %bitcast.21), calls=%async_computation.1 | async-start | bytes 16777216 | tf_op jit(solution)/shard_map/all_to_all | solution.py:37
  88.7 0.0 all-reduce.6.cloned.1.call-start
  88.8 0.0 copy-done.4
  88.8 0.1 copy.23
  88.9 0.1 reshape.169
  89.0 0.1 multiply_reduce_fusion
  89.1 0.1 and_reduce_fusion
  89.3 30.4 %scatter_custom_fusion.1 = bf16[1048576]{0:T(1024)(128)(2,1)} fusion(s32[4096]{0:T(1024)S(1)} %broadcast_select_fusion, bf16[4096]{0:T(1024)(128)(2,1)S(1)} %reshape.169, bf16[]{:T(256)} %constant.50.clone.1), kind=kCustom, calls=%fused_computation.10 | custom fusion | bytes 2097154
  119.7 2.8 reshape.150
  122.5 152.3 %all-to-all-done.1 = bf16[64,128,512]{2,1,0:T(8,128)(2,1)} async-done(((bf16[64,128,512]{2,1,0:T(8,128)(2,1)}), bf16[64,128,512]{2,1,0:T(8,128)(2,1)}, u32[]{:S(2)}, u32[]{:S(2)}) %all-to-all-start.1) | async-done | bytes 8388640 | tf_op jit(solution)/shard_map/all_to_all | solution.py:37
  274.8 7.1 %fusion.15 = f32[8192,512]{1,0:T(8,128)S(1)} fusion(bf16[8192,512]{1,0:T(8,128)(2,1)} %bitcast.5, bf16[512,512]{1,0:T(8,128)(2,1)S(1)} %copy-done), kind=kOutput, calls=%fused_computation.43 | convolution fusion | flops 4294967296 | bytes 25690112 | tf_op jit(solution)/shard_map/dot_general | solution.py:48
  281.9 0.0 copy-start.3
  281.9 0.0 copy-start.5
  281.9 1.6 fusion.3
  283.5 4.1 copy-done.1
  287.6 0.8 fusion.16
  288.4 0.0 all-reduce.6.cloned.1.call-update
  288.5 0.0 all-reduce.8.cloned.1.call-start
  288.5 42.6 %all-reduce.6.cloned.1.call-done = f32[128,256]{1,0:T(8,128)} async-done(((f32[128,256]{1,0:T(8,128)}), f32[128,256]{1,0:T(8,128)}) %all-reduce.6.cloned.1.call-update) | async-done | bytes 131088 | tf_op jit(solution)/shard_map/psum | solution.py:52
  331.1 1.0 exponential_reduce_fusion
  332.1 0.0 copy-done.5
  332.1 1.1 convolution_convert_fusion
  333.2 16.1 %fusion.2 = f32[512,512]{1,0:T(8,128)} fusion(bf16[8192,512]{1,0:T(8,128)(2,1)} %bitcast.5, f32[8192,512]{1,0:T(8,128)} %copy-done.1, bf16[128,8192]{1,0:T(8,128)(2,1)S(1)} %reshape.150, bf16[128,512]{1,0:T(8,128)(2,1)S(1)} %convolution_convert_fusion), kind=kOutput, calls=%fused_computation.7 | convolution fusion | flops 5381292032 | bytes 28442624 | tf_op jit(solution)/shard_map/dot_general | solution.py:69
  349.3 1.1 fusion.14
  350.4 0.0 all-reduce.8.cloned.1.call-update
  350.5 0.0 all-reduce.10.cloned.1.call-start
  350.5 70.9 %all-reduce.8.cloned.1.call-done = (f32[512,512]{1,0:T(8,128)}, f32[512,256]{1,0:T(8,128)}) async-done(((f32[512,512]{1,0:T(8,128)}, f32[512,256]{1,0:T(8,128)}), (f32[512,512]{1,0:T(8,128)}, f32[512,256]{1,0:T(8,128)})) %all-reduce.8.cloned.1.call-update) | async-done | bytes 1572880 | tf_op jit(solution)/shard_map/psum | solution.py:8
  421.4 0.0 all-reduce.10.cloned.1.call-update
  421.4 80.8 %all-reduce.10.cloned.1.call-done = (f32[512,512]{1,0:T(8,128)}, f32[512,256]{1,0:T(8,128)}) async-done(((f32[512,512]{1,0:T(8,128)}, f32[512,256]{1,0:T(8,128)}), (f32[512,512]{1,0:T(8,128)}, f32[512,256]{1,0:T(8,128)})) %all-reduce.10.cloned.1.call-update) | async-done | bytes 1572880 | tf_op jit(solution)/shard_map/psum | solution.py:9
  502.2 2.3 copy.29
  504.5 1.9 copy.30
  (17 shorter events, 0.1 us)
Async XLA Ops:
  7.2 267.6 %copy-start = (bf16[512,512]{1,0:T(8,128)(2,1)S(1)}, bf16[512,512]{1,0:T(8,128)(2,1)}, u32[]{:S(2)}) copy-start(bf16[512,512]{1,0:T(8,128)(2,1)} %param.10) | copy-start | bytes 1572868
  82.8 6.0 %copy-start.4 = (bf16[128,32]{0,1:T(8,128)(2,1)S(1)}, bf16[128,32]{0,1:T(8,128)(2,1)}, u32[]{:S(2)}) copy-start(bf16[128,32]{0,1:T(8,128)(2,1)} %param.8) | copy-start | bytes 24580
  82.8 6.2 %copy-start.7 = (s32[2]{0:T(128)S(1)}, s32[2]{0:T(128)}, u32[]{:S(2)}) copy-start(s32[2]{0:T(128)} %constant.51) | copy-start | bytes 28
  82.8 6.3 %copy-start.6 = (s32[2]{0:T(128)S(1)}, s32[2]{0:T(128)}, u32[]{:S(2)}) copy-start(s32[2]{0:T(128)} %constant.54) | copy-start | bytes 28
  82.8 191.9 %all-to-all-start.1 = ((bf16[64,128,512]{2,1,0:T(8,128)(2,1)}), bf16[64,128,512]{2,1,0:T(8,128)(2,1)}, u32[]{:S(2)}, u32[]{:S(2)}) async-start(bf16[64,128,512]{2,1,0:T(8,128)(2,1)} %bitcast.21), calls=%async_computation.1 | async-start | bytes 16777216 | tf_op jit(solution)/shard_map/all_to_all | solution.py:37
  88.7 242.3 %all-reduce.6.cloned.1.call-start = ((), (), s32[]{:S(2)}) async-start(), calls=%async_computation.2 | async-start | bytes 262144 | tf_op jit(solution)/shard_map/psum | solution.py:52
  281.9 5.7 %copy-start.1 = (f32[8192,512]{1,0:T(8,128)}, f32[8192,512]{1,0:T(8,128)S(1)}, u32[]{:S(2)}) copy-start(f32[8192,512]{1,0:T(8,128)S(1)} %fusion.15) | copy-start | bytes 50331652
  281.9 5.7 %copy-start.3 = (bf16[512,256]{1,0:T(8,128)(2,1)S(1)}, bf16[512,256]{1,0:T(8,128)(2,1)}, u32[]{:S(2)}) copy-start(bf16[512,256]{1,0:T(8,128)(2,1)} %param.11) | copy-start | bytes 786436
  281.9 50.2 %copy-start.5 = (s32[128]{0:T(128)S(1)}, s32[128]{0:T(128)}, u32[]{:S(2)}) copy-start(s32[128]{0:T(128)} %param.9) | copy-start | bytes 1540
  288.5 132.9 %all-reduce.8.cloned.1.call-start = ((), (), s32[]{:S(2)}) async-start(), calls=%async_computation.3 | async-start | bytes 3145728 | tf_op jit(solution)/shard_map/psum | solution.py:8
  333.2 16.1 %copy-start.2 = (f32[128,256]{1,0:T(8,128)S(1)}, f32[128,256]{1,0:T(8,128)}, u32[]{:S(2)}) copy-start(f32[128,256]{1,0:T(8,128)} %all-reduce.6.cloned.1.call-done) | copy-start | bytes 393220
  350.5 151.8 %all-reduce.10.cloned.1.call-start = ((), (), s32[]{:S(2)}) async-start(), calls=%async_computation.4 | async-start | bytes 3145728 | tf_op jit(solution)/shard_map/psum | solution.py:9
Sparse Core Ops, SparseCore 0:
  288.6 42.4 all-reduce.5
  350.6 70.7 all-reduce.7
  424.0 78.2 all-reduce.9
